TPU v7x, 32 devices: a whole 2x2x4 slice. The times are simulated.
32 devices in a mesh: pb: 8 (over y, x, core), ka: 4 (over z).
Axes of the slice: x: 2, y: 2, z: 4, core: 2. Of those that a mesh axis runs over, the one named last changes fastest.
Arguments:
- atoms: bfloat16 [24576, 128], P('pb'), may hold values from -6 to 6
- atom_gain: float32 [128], replicated, may hold values from 0.1 to 1.9
- atom_qkv: bfloat16 [128, 384], replicated, may hold values from -0.5 to 0.5
- atom_proj: bfloat16 [128, 128], replicated, may hold values from -0.5 to 0.5
- atom_bias: bfloat16 [4, 24576, 128], P(None, 'pb'), may hold values from -4 to 250
- window_shift: int32 [768], P('pb'), may hold values from -64 to -32, as said below
- token_of_atom: int32 [24576], P('pb'), may hold values from 0 to 3071, as said below
- agg_weight: bfloat16 [128, 768], replicated, may hold values from -0.5 to 0.5
- token_gain: float32 [768], replicated, may hold values from 0.1 to 1.9
- token_q: bfloat16 [768, 768], replicated, may hold values from -0.21875 to 0.21875
- token_kv: bfloat16 [768, 1536], replicated, may hold values from -0.21875 to 0.21875
- token_o: bfloat16 [768, 768], replicated, may hold values from -0.21875 to 0.21875
- pair_bias: bfloat16 [16, 3072, 3072], P(None, 'pb', 'ka'), may hold values from -4 to 250
Outputs:
- atom_out: bfloat16 [24576, 128], P('pb')
- tokens_out: bfloat16 [3072, 768], P('pb')
Inputs may be any that keep to these rules, and one draw needn't show every extreme that they name: token_of_atom never falls along the atoms and names every token at least once. Of the 3072 atoms of one index of pb, all but its last ones belong to that index's own 384 tokens; for every index but the final one, its last 192 to 384 atoms belong to the tokens of the index after, and the final index's atoms are all its own. In every draw some index has all of its last 384 atoms in the index after. The key window of query block b begins at atom 32 b + window_shift[b]; both ends of the range occur in every draw.
All inputs are finite; a program needn't handle non-finite values.
Results may differ from a plain program's by a relative error of at most 0.0095.
Values may be sent and summed in bfloat16 or wider, within the bound.
No kernel may reach another device: no remote copies, remote signals or barrier semaphores. Data moves between devices by JAX's collectives and lax.ppermute only.
A program may use at most 128 MiB of HBM per device.

v0:
```python
import functools
import math

import jax
import jax.numpy as jnp
from jax import lax
from jax.experimental import pallas as pl
from jax.experimental.pallas import tpu as pltpu
from jax.sharding import PartitionSpec as P

AH = 4
TH = 16
WIN_Q = 32
WIN_K = 128
SHIFT_MAX = 384
LANES = 128
F32 = jnp.float32
BF16 = jnp.bfloat16
VMEM_LIMIT = 56 * 1024 * 1024
VMEM_SMALL = 24 * 1024 * 1024


def full(shape):
    return pl.BlockSpec(shape, lambda *_: (0,) * len(shape))


def params(limit=VMEM_LIMIT):
    return pltpu.CompilerParams(vmem_limit_bytes=limit)


def norm_rows(as_float, gain):
    centre = jnp.mean(as_float, axis=-1, keepdims=True)
    spread = jnp.mean(jnp.square(as_float - centre), axis=-1, keepdims=True)
    return (as_float - centre) * lax.rsqrt(spread + 1e-05) * gain


def dot(a, b):
    return jnp.dot(a, b, preferred_element_type=F32)


def dot_nt(a, b):
    return lax.dot_general(a, b, (((1,), (1,)), ((), ())), preferred_element_type=F32)


def atom_kernel(
    chunks,
    atom_total,
    tok_rows,
    shift_ref,
    pos_ref,
    atoms_ref,
    left_ref,
    right_ref,
    gain_ref,
    qkv_ref,
    proj_ref,
    bias_ref,
    tok_ref,
    out_ref,
    msg_ref,
    q_s,
    k_s,
    v_s,
):
    step = pl.program_id(0)
    rows, width = atoms_ref.shape
    size = out_ref.shape[0]
    half = WIN_K // 2
    head = width // AH
    shard = pos_ref[0]

    @pl.when(step == 0)
    def _():
        gain = gain_ref[...]

        def project(values):
            normed = norm_rows(values.astype(F32), gain).astype(BF16)
            return dot(normed, qkv_ref[...])

        def keep(res, at, count):
            k_s[pl.ds(at, count), :] = res[:, width : 2 * width].astype(BF16)
            v_s[pl.ds(at, count), :width] = res[:, 2 * width :].astype(BF16)
            v_s[pl.ds(at, count), width:] = jnp.ones((count, width), BF16)

        def one(c, carry):
            at = pl.multiple_of(c * size, size)
            res = project(atoms_ref[pl.ds(at, size), :])
            q_s[pl.ds(at, size), :] = (res[:, :width] * (1.0 / math.sqrt(head))).astype(BF16)
            keep(res, pl.multiple_of(at + half, half), size)
            return carry

        lax.fori_loop(0, chunks, one, 0, unroll=2)
        keep(project(left_ref[...]), 0, half)
        keep(project(right_ref[...]), half + rows, half)

    group = WIN_K // WIN_Q
    atoms_group = group * WIN_Q
    lane_q = lax.broadcasted_iota(jnp.int32, (WIN_Q, width), 1)
    heads = [(lane_q >= h * head) & (lane_q < (h + 1) * head) for h in range(AH)]
    lane = lax.broadcasted_iota(jnp.int32, (AH * WIN_Q, WIN_K), 1)
    slot = lax.broadcasted_iota(jnp.int32, (1, WIN_K), 1)
    for g in range(size // atoms_group):
        local = g * atoms_group
        at = pl.multiple_of(step * size + local, atoms_group)
        keys = k_s[pl.ds(at, 2 * WIN_K), :]
        values = v_s[pl.ds(at, 2 * WIN_K), :]
        query = q_s[pl.ds(at, atoms_group), :].astype(F32)
        stacked = jnp.concatenate(
            [
                jnp.where(m, query[i * WIN_Q : (i + 1) * WIN_Q], 0.0).astype(BF16)
                for i in range(group)
                for m in heads
            ],
            axis=0,
        )
        scores = dot_nt(stacked, keys)
        weights = []
        for i in range(group):
            offset = i * WIN_Q + half + shift_ref[(step * size + local) // WIN_Q + i]
            early = lane >= offset
            span = AH * WIN_Q
            mine = scores[i * span : (i + 1) * span]
            begin = local + i * WIN_Q
            bias = bias_ref[:, begin : begin + WIN_Q, :].astype(F32).reshape(span, WIN_K)
            index = slot + jnp.where(slot >= offset, 0, WIN_K) + (at + shard * rows - half)
            shut = jnp.where((index >= 0) & (index < atom_total), 0.0, -jnp.inf)
            logits = jnp.where(early, mine[:, :WIN_K], mine[:, WIN_K:]) + (
                pltpu.roll(bias, jnp.bitwise_and(offset, WIN_K - 1), 1) + shut
            )
            terms = jnp.exp(logits - jnp.max(logits, axis=-1, keepdims=True))
            weights.append(
                jnp.concatenate(
                    [jnp.where(early, terms, 0.0).astype(BF16), jnp.where(early, 0.0, terms).astype(BF16)],
                    axis=1,
                )
            )
        mixed = dot(jnp.concatenate(weights, axis=0), values)
        merged = []
        for i in range(group):
            acc = None
            for h in range(AH):
                top = (i * AH + h) * WIN_Q
                part = mixed[top : top + WIN_Q]
                acc = part if acc is None else jnp.where(jnp.concatenate([heads[h]] * 2, axis=1), part, acc)
            merged.append((acc[:, :width] / acc[:, width:]).astype(BF16))
        own = atoms_ref[pl.ds(at, atoms_group), :].astype(F32)
        result = own + dot(jnp.concatenate(merged, axis=0), proj_ref[...])
        out_ref[local : local + atoms_group, :] = result.astype(BF16)

    @pl.when(step == chunks - 1)
    def _():
        ids = tok_ref[tok_ref.shape[0] - 8 :, :]
        code = jnp.maximum(ids - (shard + 1) * tok_rows + 1, 0)
        high = (code >> 4).astype(F32)
        low = (code & 15).astype(F32)
        msg_ref[:size, :] = out_ref[...]
        msg_ref[size:, :] = jnp.concatenate([high, low], axis=0).astype(BF16)


def atom_attention(shift, pos, atoms, left, right, gain, qkv, proj, bias, tok2d, tok_rows, atom_total):
    rows, width = atoms.shape
    size = SHIFT_MAX
    chunks = rows // size
    half = WIN_K // 2
    return pl.pallas_call(
        functools.partial(atom_kernel, chunks, atom_total, tok_rows),
        grid_spec=pltpu.PrefetchScalarGridSpec(
            num_scalar_prefetch=2,
            grid=(chunks,),
            in_specs=[
                full((rows, width)),
                full((half, width)),
                full((half, width)),
                full((1, width)),
                full(qkv.shape),
                full(proj.shape),
                pl.BlockSpec((AH, size, WIN_K), lambda i, *_: (0, i, 0)),
                full(tok2d.shape),
            ],
            out_specs=[
                pl.BlockSpec((size, width), lambda i, *_: (i, 0)),
                full((size + 16, width)),
            ],
            scratch_shapes=[
                pltpu.VMEM((rows, width), BF16),
                pltpu.VMEM((rows + 2 * half, width), BF16),
                pltpu.VMEM((rows + 2 * half, 2 * width), BF16),
            ],
        ),
        out_shape=[
            jax.ShapeDtypeStruct((rows, width), BF16),
            jax.ShapeDtypeStruct((size + 16, width), BF16),
        ],
        compiler_params=params(),
        cost_estimate=pl.CostEstimate(flops=8 * 10**9, bytes_accessed=6 * 10**6, transcendentals=2 * 10**6),
        name="atom_attention",
    )(shift, pos, atoms, left, right, gain, qkv, proj, bias, tok2d)


def activate(rows, weight_half):
    u = dot(rows, weight_half)
    return (u + u * jnp.tanh(u)).astype(BF16)


def pool_kernel(tok_rows, pos_ref, out_ref, weight_ref, tok_ref, sum_ref, cnt_ref):
    step = pl.program_id(0)
    size = out_ref.shape[0]
    lines = size // LANES
    base = pos_ref[0] * tok_rows
    token = lax.broadcasted_iota(jnp.int32, (tok_rows, LANES), 0)
    weight_half = (weight_ref[...].astype(F32) * 0.5).astype(BF16)
    hidden = activate(out_ref[...], weight_half)
    ones = []
    for j in range(lines):
        ids = tok_ref[pl.ds(step * lines + j, 1), :] - base
        ones.append(jnp.where(token == ids, 1.0, 0.0))
    hot = jnp.concatenate(ones, axis=1).astype(BF16)
    count = functools.reduce(jnp.add, ones)
    part = dot(hot, hidden)

    @pl.when(step == 0)
    def _():
        sum_ref[...] = part
        cnt_ref[...] = count

    @pl.when(step > 0)
    def _():
        sum_ref[...] += part
        cnt_ref[...] += count


def pool(pos, atom_out, weight, tok2d, tok_rows):
    rows, width = atom_out.shape
    feats = weight.shape[1]
    size = 512
    return pl.pallas_call(
        functools.partial(pool_kernel, tok_rows),
        grid_spec=pltpu.PrefetchScalarGridSpec(
            num_scalar_prefetch=1,
            grid=(rows // size,),
            in_specs=[
                pl.BlockSpec((size, width), lambda i, *_: (i, 0)),
                full(weight.shape),
                full(tok2d.shape),
            ],
            out_specs=[full((tok_rows, feats)), full((tok_rows, LANES))],
        ),
        out_shape=[
            jax.ShapeDtypeStruct((tok_rows, feats), F32),
            jax.ShapeDtypeStruct((tok_rows, LANES), F32),
        ],
        compiler_params=params(),
        cost_estimate=pl.CostEstimate(flops=4 * 10**9, bytes_accessed=3 * 10**6, transcendentals=2 * 10**6),
        name="pool",
    )(pos, atom_out, weight, tok2d)


def finish_kernel(msg_ref, weight_ref, sum_ref, cnt_ref, gain_ref, repr_ref, normed_ref):
    tok_rows = sum_ref.shape[0]
    size = msg_ref.shape[0] - 16
    lines = size // LANES
    token = lax.broadcasted_iota(jnp.int32, (tok_rows, LANES), 0).astype(F32)
    weight_half = (weight_ref[...].astype(F32) * 0.5).astype(BF16)
    hidden = activate(msg_ref[:size, :], weight_half)
    codes = msg_ref[size:, :].astype(F32)
    ids = codes[:8] * 16.0 + codes[8:] - 1.0
    ones = [jnp.where(token == ids[8 - lines + j : 9 - lines + j], 1.0, 0.0) for j in range(lines)]
    hot = jnp.concatenate(ones, axis=1).astype(BF16)
    count = functools.reduce(jnp.add, ones) + cnt_ref[...]
    sums = sum_ref[...] + dot(hot, hidden)
    token_repr = (sums / jnp.sum(count, axis=1, keepdims=True)).astype(BF16)
    repr_ref[...] = token_repr
    normed_ref[...] = norm_rows(token_repr.astype(F32), gain_ref[...]).astype(BF16)


def finish(msg, weight, sums, counts, gain):
    shape = sums.shape
    return pl.pallas_call(
        finish_kernel,
        out_shape=[jax.ShapeDtypeStruct(shape, BF16)] * 2,
        compiler_params=params(VMEM_SMALL),
        cost_estimate=pl.CostEstimate(flops=4 * 10**8, bytes_accessed=3 * 10**6, transcendentals=3 * 10**5),
        name="token_finish",
    )(msg, weight, sums, counts, gain)


HEADS_STEP = 8


def pack_lse(lse):
    lane = lax.broadcasted_iota(jnp.int32, lse.shape, 1)
    high = lse.astype(BF16).astype(F32)
    rest = lse - high
    middle = rest.astype(BF16).astype(F32)
    low = rest - middle
    return jnp.where(
        lane < TH,
        high,
        jnp.where(lane < 2 * TH, pltpu.roll(middle, TH, 1), pltpu.roll(low, 2 * TH, 1)),
    ).astype(BF16)


def unpack_lse(coded):
    value = coded.astype(F32)
    return value + pltpu.roll(value, LANES - TH, 1) + pltpu.roll(value, LANES - 2 * TH, 1)


def attend_step(step, half, q_ref, k_ref, v_ref, bias_ref, o_s, lse_s):
    rows = o_s.shape[0]
    width = q_ref.shape[1] // TH
    span = HEADS_STEP * width
    at = pl.multiple_of(half * rows, rows)
    spot = lax.broadcasted_iota(jnp.int32, (rows, LANES), 1)
    lse = lse_s[...]
    for p in range(HEADS_STEP // 2):
        first = 2 * p * width
        low = first // LANES * LANES
        wide = -(-(first + 2 * width) // LANES) * LANES - low
        first -= low
        free = 0 if first >= 16 else 2 * width
        window = pl.ds(pl.multiple_of(step * span + low, LANES), wide)
        lane = lax.broadcasted_iota(jnp.int32, (rows, wide), 1)
        masks = [(lane >= first + j * width) & (lane < first + (j + 1) * width) for j in range(2)]
        query = q_ref[pl.ds(at, rows), window].astype(F32)
        stacked = jnp.concatenate([jnp.where(m, query, 0.0).astype(BF16) for m in masks], axis=0)
        bias = bias_ref[2 * p : 2 * p + 2].astype(F32)
        scores = dot_nt(stacked, k_ref[:, window]) + bias.reshape(2 * rows, bias.shape[2])
        top = jnp.max(scores, axis=-1, keepdims=True)
        terms = jnp.exp(scores - top).astype(BF16)
        values = v_ref[:, window]
        column = lax.broadcasted_iota(jnp.int32, values.shape, 1)
        used = (column >= first) & (column < first + 2 * width)
        mixed = dot(terms, jnp.where(used, values.astype(F32), 1.0).astype(BF16))
        total = mixed[:, free : free + 1]
        mixed = mixed / total
        sums = top + jnp.log(total)
        result = o_s[:, window]
        for j in range(2):
            result = jnp.where(masks[j], mixed[j * rows : (j + 1) * rows], result)
            lse = jnp.where(spot == step * HEADS_STEP + 2 * p + j, sums[j * rows : (j + 1) * rows], lse)
        o_s[:, window] = result
    lse_s[...] = lse


def send_kernel(steps, half_ref, core_ref, q_ref, own_ref, other_ref, wkv_ref, bias_ref, k_ref, v_ref, msg_ref, o_s, lse_s, x_s):
    step = pl.program_id(0)
    rows, feats = own_ref.shape

    @pl.when(step == 0)
    def _():
        core = core_ref[0]
        x_s[pl.ds(pl.multiple_of(core * rows, rows), rows), :] = own_ref[...]
        x_s[pl.ds(pl.multiple_of((1 - core) * rows, rows), rows), :] = other_ref[...]
        for r in range(0, 2 * rows, rows):
            k_ref[r : r + rows, :] = dot(x_s[r : r + rows, :], wkv_ref[:, :feats]).astype(BF16)
            v_ref[r : r + rows, :] = dot(x_s[r : r + rows, :], wkv_ref[:, feats:]).astype(BF16)
        lse_s[...] = jnp.zeros_like(lse_s)

    attend_step(step, half_ref[0], q_ref, k_ref, v_ref, bias_ref, o_s, lse_s)

    @pl.when(step == steps - 1)
    def _():
        msg_ref[:, :feats] = o_s[...].astype(BF16)
        msg_ref[:, feats:] = pack_lse(lse_s[...])


def keep_kernel(half_ref, q_ref, k_ref, v_ref, bias_ref, o_ref, lse_ref):
    step = pl.program_id(0)

    @pl.when(step == 0)
    def _():
        lse_ref[...] = jnp.zeros_like(lse_ref)

    attend_step(step, half_ref[0], q_ref, k_ref, v_ref, bias_ref, o_ref, lse_ref)


def attention(half, q, bias, keys, first):
    tok_rows, feats = q.shape
    rows = tok_rows // 2
    key_rows = bias.shape[2]
    steps = TH // HEADS_STEP
    bias_spec = pl.BlockSpec((HEADS_STEP, rows, key_rows), lambda i, s, *_: (i, s[0], 0))
    kv_shape = (key_rows, feats)
    cost = pl.CostEstimate(flops=8 * 10**9, bytes_accessed=8 * 10**6, transcendentals=3 * 10**6)
    if first:
        core, own, other, wkv = keys
        return pl.pallas_call(
            functools.partial(send_kernel, steps),
            grid_spec=pltpu.PrefetchScalarGridSpec(
                num_scalar_prefetch=2,
                grid=(steps,),
                in_specs=[full(q.shape), full(own.shape), full(other.shape), full(wkv.shape), bias_spec],
                out_specs=[full(kv_shape), full(kv_shape), full((rows, feats + LANES))],
                scratch_shapes=[
                    pltpu.VMEM((rows, feats), F32),
                    pltpu.VMEM((rows, LANES), F32),
                    pltpu.VMEM(kv_shape, BF16),
                ],
            ),
            out_shape=[
                jax.ShapeDtypeStruct(kv_shape, BF16),
                jax.ShapeDtypeStruct(kv_shape, BF16),
                jax.ShapeDtypeStruct((rows, feats + LANES), BF16),
            ],
            compiler_params=params(),
            cost_estimate=cost,
            name="attend_send",
        )(half, core, q, own, other, wkv, bias)
    k, v = keys
    return pl.pallas_call(
        keep_kernel,
        grid_spec=pltpu.PrefetchScalarGridSpec(
            num_scalar_prefetch=1,
            grid=(steps,),
            in_specs=[full(q.shape), full(kv_shape), full(kv_shape), bias_spec],
            out_specs=[full((rows, feats)), full((rows, LANES))],
        ),
        out_shape=[
            jax.ShapeDtypeStruct((rows, feats), F32),
            jax.ShapeDtypeStruct((rows, LANES), F32),
        ],
        compiler_params=params(),
        cost_estimate=cost,
        name="attend_keep",
    )(half, q, k, v, bias)


def merged_rows(o_ref, lse_ref, msg_ref):
    rows, feats = o_ref.shape
    width = feats // TH
    other = msg_ref[:, :feats].astype(F32)
    lse_b = unpack_lse(msg_ref[:, feats:])
    spot = lax.broadcasted_iota(jnp.int32, (rows, LANES), 1)
    lse_a = lse_ref[...]
    lse_b = jnp.where(spot < TH, lse_b, lse_a)
    top = jnp.maximum(lse_a, lse_b)
    part_a = jnp.exp(lse_a - top)
    total = part_a + jnp.exp(lse_b - top)
    share = part_a / total
    high = share.astype(BF16)
    low = (share - high.astype(F32)).astype(BF16)
    head = lax.broadcasted_iota(jnp.int32, (LANES, feats), 0) * width
    column = lax.broadcasted_iota(jnp.int32, (LANES, feats), 1)
    spread = jnp.where((column >= head) & (column < head + width), 1.0, 0.0).astype(BF16)
    wide = dot(high, spread) + dot(low, spread)
    return other + wide * (o_ref[...] - other), top + jnp.log(total)


def merge_kernel(o_ref, lse_ref, msg_ref, out_ref, sum_ref, back_ref):
    mixed, lse = merged_rows(o_ref, lse_ref, msg_ref)
    feats = mixed.shape[1]
    out_ref[...] = mixed
    sum_ref[...] = lse
    back_ref[:, :feats] = mixed.astype(BF16)
    back_ref[:, feats:] = pack_lse(lse)


def merge(o, lse, msg):
    return pl.pallas_call(
        merge_kernel,
        out_shape=[
            jax.ShapeDtypeStruct(o.shape, F32),
            jax.ShapeDtypeStruct(lse.shape, F32),
            jax.ShapeDtypeStruct(msg.shape, BF16),
        ],
        compiler_params=params(VMEM_SMALL),
        name="merge",
    )(o, lse, msg)


def last_kernel(half_ref, o_ref, lse_ref, msg_ref, repr_ref, weight_ref, out_ref):
    rows = o_ref.shape[0]
    mixed, _ = merged_rows(o_ref, lse_ref, msg_ref)
    own = repr_ref[pl.ds(pl.multiple_of(half_ref[0] * rows, rows), rows), :].astype(F32)
    out_ref[...] = (own + dot(mixed.astype(BF16), weight_ref[...])).astype(BF16)


def last_merge(half, o, lse, msg, token_repr, weight):
    return pl.pallas_call(
        last_kernel,
        in_specs=[pl.BlockSpec(memory_space=pltpu.SMEM)] + [pl.BlockSpec(memory_space=pltpu.VMEM)] * 5,
        out_shape=jax.ShapeDtypeStruct(o.shape, BF16),
        compiler_params=params(VMEM_SMALL),
        name="merge_last",
    )(half, o, lse, msg, token_repr, weight)


def join_kernel(half_ref, own_ref, other_ref, out_ref):
    rows = own_ref.shape[0]
    out_ref[pl.ds(pl.multiple_of(half_ref[0] * rows, rows), rows), :] = own_ref[...]
    out_ref[pl.ds(pl.multiple_of((1 - half_ref[0]) * rows, rows), rows), :] = other_ref[...]


def join(half, own, other):
    rows, feats = own.shape
    return pl.pallas_call(
        join_kernel,
        in_specs=[pl.BlockSpec(memory_space=pltpu.SMEM)] + [pl.BlockSpec(memory_space=pltpu.VMEM)] * 2,
        out_shape=jax.ShapeDtypeStruct((2 * rows, feats), BF16),
        compiler_params=params(VMEM_SMALL),
        name="join",
    )(half, own, other)


def bits_of(count):
    return [1 << b for b in range(count.bit_length() - 1)]


def key_block(normed):
    n_pb, n_ka = lax.axis_size("pb"), lax.axis_size("ka")
    cores = n_pb // n_ka
    chips = n_pb // cores
    shard, plane = lax.axis_index("pb"), lax.axis_index("ka")
    bits = bits_of(chips)
    core = lax.rem(shard, cores)
    away = jnp.bitwise_xor(shard // cores, plane)
    held = normed
    for r in range(len(bits)):
        pairs = []
        gets = jnp.bool_(False)
        for c in range(cores):
            order = bits if c % 2 == 0 else bits[::-1]
            known = sum(order[:r])
            for k in range(n_ka):
                for j in range(chips):
                    if (j ^ k) & ~known == 0:
                        pairs.append(((j * cores + c) * n_ka + k, ((j ^ order[r]) * cores + c) * n_ka + k))
            fresh = (jnp.bitwise_and(away, ~(known + order[r])) == 0) & (jnp.bitwise_and(away, order[r]) != 0)
            gets = gets | (fresh & (core == c))
        moved = lax.ppermute(held, ("pb", "ka"), pairs)
        held = jnp.where(gets, moved, held)
    swap = [(p, p ^ 1) for p in range(n_pb)]
    return held, lax.ppermute(held, "pb", swap)


def body(
    atoms,
    atom_gain,
    atom_qkv,
    atom_proj,
    atom_bias,
    window_shift,
    token_of_atom,
    agg_weight,
    token_gain,
    token_q,
    token_kv,
    token_o,
    pair_bias,
):
    n_pb, n_ka = lax.axis_size("pb"), lax.axis_size("ka")
    shard, plane = lax.axis_index("pb"), lax.axis_index("ka")
    rows, width = atoms.shape
    tok_rows = pair_bias.shape[1]
    half = WIN_K // 2
    up = [(i, i + 1) for i in range(n_pb - 1)]
    down = [(i + 1, i) for i in range(n_pb - 1)]
    pos = shard.astype(jnp.int32).reshape(1)
    tok2d = token_of_atom.reshape(rows // LANES, LANES)
    left = lax.ppermute(atoms[rows - half :], "pb", up)
    right = lax.ppermute(atoms[:half], "pb", down)
    atom_out, msg = atom_attention(
        window_shift, pos, atoms, left, right, atom_gain.reshape(1, width), atom_qkv, atom_proj,
        atom_bias, tok2d, tok_rows, rows * n_pb,
    )
    behind = lax.ppermute(msg, "pb", up)
    sums, counts = pool(pos, atom_out, agg_weight, tok2d, tok_rows)
    token_repr, normed = finish(behind, agg_weight, sums, counts, token_gain.reshape(1, -1))
    own_keys, other_keys = key_block(normed)
    scale = 1.0 / math.sqrt(token_q.shape[1] // TH)
    queries = (dot(normed, token_q) * scale).astype(BF16)
    parity = lax.rem(plane, 2).astype(jnp.int32)
    core = lax.rem(shard, n_pb // n_ka).astype(jnp.int32)
    k, v, near = attention(
        (1 - parity).reshape(1), queries, pair_bias, (core.reshape(1), own_keys, other_keys, token_kv), True
    )
    got = lax.ppermute(near, "ka", [(i, i ^ 1) for i in range(n_ka)])
    o, lse = attention(parity.reshape(1), queries, pair_bias, (k, v), False)
    for bit in bits_of(n_ka)[1:]:
        o, lse, far = merge(o, lse, got)
        got = lax.ppermute(far, "ka", [(i, i ^ bit) for i in range(n_ka)])
    part = last_merge(parity.reshape(1), o, lse, got, token_repr, token_o)
    rest = lax.ppermute(part, "ka", [(i, i ^ 1) for i in range(n_ka)])
    return atom_out, join(parity.reshape(1), part, rest)


def solution(mesh):
    return jax.shard_map(
        body,
        mesh=mesh,
        in_specs=(
            P("pb", None),
            P(),
            P(),
            P(),
            P(None, "pb", None),
            P("pb"),
            P("pb"),
            P(),
            P(),
            P(),
            P(),
            P(),
            P(None, "pb", "ka"),
        ),
        out_specs=(P("pb", None), P("pb", None)),
        check_vma=False,
    )
```

profile of v0, /device:TPU:0, one launch (start us, length us, event | category | flops | bytes accessed | tf_op | source)
XLA Modules:
  0.0 123.9 jit_solution(14941441586285866703)
XLA Ops:
  0.6 0.8 fusion.1
  1.5 1.3 %collective-permute-start.1 = (bf16[64,128]{1,0:T(8,128)(2,1)S(1)}, bf16[64,128]{1,0:T(8,128)(2,1)S(1)}, u32[]{:S(2)}, u32[]{:S(2)}) collective-permute-start(bf16[64,128]{1,0:T(8,128)(2,1)S(1)} %get-tuple-element.30), channel_id=1, source_target_pairs={{4,0},{8,4},{12,8},{16,12},{20,16},{24,20},{28,24},{5,1},{9,5},{13... | collective-permute-start | bytes 49160 | tf_op jit(solution)/shard_map/ppermute | solution.py:561
  2.8 3.0 %collective-permute-start = (bf16[64,128]{1,0:T(8,128)(2,1)S(1)}, bf16[64,128]{1,0:T(8,128)(2,1)S(1)}, u32[]{:S(2)}, u32[]{:S(2)}) collective-permute-start(bf16[64,128]{1,0:T(8,128)(2,1)S(1)} %get-tuple-element.31), channel_id=1, source_target_pairs={{0,4},{4,8},{8,12},{12,16},{16,20},{20,24},{24,28},{1,5},{5,9},{9,... | collective-permute-start | bytes 49160 | tf_op jit(solution)/shard_map/ppermute | solution.py:560
  5.8 0.7 reshape.31.gain_ref
  6.6 0.5 copy-done.9
  7.1 0.1 copy-done.10
  7.2 20.4 %atom_attention.1 = (bf16[3072,128]{1,0:T(8,128)(2,1)}, bf16[400,128]{1,0:T(8,128)(2,1)}) custom-call(s32[96]{0:T(128)} %shift_ref.1, s32[1]{0:T(128)} %bitcast.pos_ref, bf16[3072,128]{1,0:T(8,128)(2,1)} %atoms_ref.1, bf16[64,128]{1,0:T(8,128)(2,1)} %copy-done.10, bf16[64,128]{1,0:T(8,128)(2,1)} %copy-done.9, f32[1,128]{1,0:T(1,128)} %bitcast.10, ...), custom_call_target="tpu_custom_call" | custom-call | flops 8000000000 | bytes 6000000 | tf_op jit(solution)/shard_map/atom_attention/pallas_call | solution.py:165
  27.6 4.5 %collective-permute-start.2 = (bf16[400,128]{1,0:T(8,128)(2,1)}, bf16[400,128]{1,0:T(8,128)(2,1)S(1)}, u32[]{:S(2)}, u32[]{:S(2)}) collective-permute-start(bf16[400,128]{1,0:T(8,128)(2,1)} %get-tuple-element.17), channel_id=1, source_target_pairs={{0,4},{4,8},{8,12},{12,16},{16,20},{20,24},{24,28},{1,5},{5,9},{9,... | collective-permute-start | bytes 307208 | tf_op jit(solution)/shard_map/ppermute | solution.py:566
  32.1 7.9 %pool.1 = (f32[384,768]{1,0:T(8,128)}, f32[384,128]{1,0:T(8,128)}) custom-call(s32[1]{0:T(128)} %bitcast.pos_ref, bf16[3072,128]{1,0:T(8,128)(2,1)} %get-tuple-element.14.out_ref, bf16[128,768]{1,0:T(8,128)(2,1)} %weight_ref.4, s32[24,128]{1,0:T(8,128)} %bitcast.9), custom_call_target="tpu_custom_call" | custom-call | flops 4000000000 | bytes 3000000 | tf_op jit(solution)/shard_map/pool/pallas_call | solution.py:236
  40.0 1.3 %copy-done.2 = f32[384,768]{1,0:T(8,128)S(1)} copy-done((f32[384,768]{1,0:T(8,128)S(1)}, f32[384,768]{1,0:T(8,128)}, u32[]{:S(2)}) %copy-start.2) | copy-done | bytes 1179672
  41.3 0.9 copy-done.5
  42.2 1.1 token_finish.1
  43.3 4.3 %collective-permute-start.3 = (bf16[384,768]{1,0:T(8,128)(2,1)S(1)}, bf16[384,768]{1,0:T(8,128)(2,1)S(1)}, u32[]{:S(2)}, u32[]{:S(2)}) collective-permute-start(bf16[384,768]{1,0:T(8,128)(2,1)S(1)} %get-tuple-element.20), channel_id=1, source_target_pairs={{0,8},{9,1},{18,26},{27,19},{4,20},{13,29},{22,6},{31,15}} | collective-permute-start | bytes 1769480 | tf_op jit(solution)/shard_map/ppermute | solution.py:530
  47.6 7.3 %collective-permute-done.3 = bf16[384,768]{1,0:T(8,128)(2,1)S(1)} collective-permute-done((bf16[384,768]{1,0:T(8,128)(2,1)S(1)}, bf16[384,768]{1,0:T(8,128)(2,1)S(1)}, u32[]{:S(2)}, u32[]{:S(2)}) %collective-permute-start.3) | collective-permute-done | bytes 589856 | tf_op jit(solution)/shard_map/ppermute | solution.py:530
  55.0 2.2 %collective-permute-start.4 = (bf16[384,768]{1,0:T(8,128)(2,1)S(1)}, bf16[384,768]{1,0:T(8,128)(2,1)}, u32[]{:S(2)}, u32[]{:S(2)}) collective-permute-start(bf16[384,768]{1,0:T(8,128)(2,1)S(1)} %broadcast_select_fusion), channel_id=1, source_target_pairs={{0,16},{8,24},{1,17},{9,25},{18,2},{26,10},{19,3},{27,11},{4,12},{... | collective-permute-start | bytes 1769480 | tf_op jit(solution)/shard_map/ppermute | solution.py:530
  57.2 6.5 %collective-permute-done.4 = bf16[384,768]{1,0:T(8,128)(2,1)} collective-permute-done((bf16[384,768]{1,0:T(8,128)(2,1)S(1)}, bf16[384,768]{1,0:T(8,128)(2,1)}, u32[]{:S(2)}, u32[]{:S(2)}) %collective-permute-start.4) | collective-permute-done | bytes 589856 | tf_op jit(solution)/shard_map/ppermute | solution.py:530
  63.9 1.4 %fusion.q_ref = bf16[384,768]{1,0:T(8,128)(2,1)} fusion(bf16[384,768]{1,0:T(8,128)(2,1)S(1)} %get-tuple-element.20, bf16[768,768]{1,0:T(8,128)(2,1)S(1)} %copy-done), kind=kOutput, calls=%fused_computation.1 | convolution fusion | flops 453574656 | bytes 2359296 | tf_op jit(solution)/shard_map/dot_general | solution.py:38
  65.3 0.5 collective-permute-done.5.other_ref
  65.9 0.8 copy-done.8
  66.7 11.2 %attend_send.1 = (bf16[768,768]{1,0:T(8,128)(2,1)}, bf16[768,768]{1,0:T(8,128)(2,1)}, bf16[192,896]{1,0:T(8,128)(2,1)}) custom-call(s32[1]{0:T(128)} %bitcast.4.half_ref, s32[1]{0:T(128)} %bitcast.5.core_ref, bf16[384,768]{1,0:T(8,128)(2,1)} %fusion.q_ref, bf16[384,768]{1,0:T(8,128)(2,1)} %copy-done.7, bf16[384,768]{1,0:T(8,128)(2,1)} %copy-done.8, ...), custom_call_target="tpu_custom_call" | custom-call | flops 8000000000 | bytes 8000000 | tf_op jit(solution)/shard_map/attend_send/pallas_call | solution.py:387
  77.9 4.0 %collective-permute-start.6 = (bf16[192,896]{1,0:T(8,128)(2,1)}, bf16[192,896]{1,0:T(8,128)(2,1)S(1)}, u32[]{:S(2)}, u32[]{:S(2)}) collective-permute-start(bf16[192,896]{1,0:T(8,128)(2,1)} %get-tuple-element.25), channel_id=1, source_target_pairs={{0,1},{1,0},{2,3},{3,2},{4,5},{5,4},{6,7},{7,6},{8,9},{9,8},{10,11... | collective-permute-start | bytes 1032200 | tf_op jit(solution)/shard_map/ppermute | solution.py:577
  81.9 8.1 %attend_keep.1 = (f32[192,768]{1,0:T(8,128)}, f32[192,128]{1,0:T(8,128)}) custom-call(s32[1]{0:T(128)} %bitcast.3.half_ref, bf16[384,768]{1,0:T(8,128)(2,1)} %fusion.q_ref, bf16[768,768]{1,0:T(8,128)(2,1)} %get-tuple-element.21.k_ref, bf16[768,768]{1,0:T(8,128)(2,1)} %get-tuple-element.22.v_ref, bf16[16,384,768]{2,1,0:T(8,128)(2,1)} %bias_ref.5), custom_call_target="tpu_custom_call" | custom-call | flops 8000000000 | bytes 8000000 | tf_op jit(solution)/shard_map/attend_keep/pallas_call | solution.py:410
  89.9 0.7 collective-permute-done.6.msg_ref
  90.7 1.1 copy-done.3
  91.7 0.9 copy-done.6
  92.6 0.5 merge.1
  93.1 5.7 %collective-permute-start.7 = (bf16[192,896]{1,0:T(8,128)(2,1)S(1)}, bf16[192,896]{1,0:T(8,128)(2,1)S(1)}, u32[]{:S(2)}, u32[]{:S(2)}) collective-permute-start(bf16[192,896]{1,0:T(8,128)(2,1)S(1)} %get-tuple-element.28), channel_id=1, source_target_pairs={{0,2},{1,3},{2,0},{3,1},{4,6},{5,7},{6,4},{7,5},{8,10},{9,11},{10,... | collective-permute-start | bytes 1032200 | tf_op jit(solution)/shard_map/ppermute | solution.py:581
  98.8 15.2 %collective-permute-done.7.msg_ref = bf16[192,896]{1,0:T(8,128)(2,1)S(1)} collective-permute-done((bf16[192,896]{1,0:T(8,128)(2,1)S(1)}, bf16[192,896]{1,0:T(8,128)(2,1)S(1)}, u32[]{:S(2)}, u32[]{:S(2)}) %collective-permute-start.7) | collective-permute-done | bytes 344096 | tf_op jit(solution)/shard_map/ppermute | solution.py:581
  114.1 0.8 merge_last.1.own_ref
  114.9 0.8 collective-permute-start.8
  115.6 7.4 %collective-permute-done.8.other_ref = bf16[192,768]{1,0:T(8,128)(2,1)S(1)} collective-permute-done((bf16[192,768]{1,0:T(8,128)(2,1)S(1)}, bf16[192,768]{1,0:T(8,128)(2,1)S(1)}, u32[]{:S(2)}, u32[]{:S(2)}) %collective-permute-start.8) | collective-permute-done | bytes 294944 | tf_op jit(solution)/shard_map/ppermute | solution.py:583
  123.0 0.9 join.1
  (21 shorter events, 0.4 us)
Async XLA Ops:
  0.6 63.3 %copy-start = (bf16[768,768]{1,0:T(8,128)(2,1)S(1)}, bf16[768,768]{1,0:T(8,128)(2,1)}, u32[]{:S(2)}) copy-start(bf16[768,768]{1,0:T(8,128)(2,1)} %param.22) | copy-start | bytes 3538948
  1.5 5.0 %collective-permute-start.1 = (bf16[64,128]{1,0:T(8,128)(2,1)S(1)}, bf16[64,128]{1,0:T(8,128)(2,1)S(1)}, u32[]{:S(2)}, u32[]{:S(2)}) collective-permute-start(bf16[64,128]{1,0:T(8,128)(2,1)S(1)} %get-tuple-element.30), channel_id=1, source_target_pairs={{4,0},{8,4},{12,8},{16,12},{20,16},{24,20},{28,24},{5,1},{9,5},{13... | collective-permute-start | bytes 49160 | tf_op jit(solution)/shard_map/ppermute | solution.py:561
  2.8 3.9 %collective-permute-start = (bf16[64,128]{1,0:T(8,128)(2,1)S(1)}, bf16[64,128]{1,0:T(8,128)(2,1)S(1)}, u32[]{:S(2)}, u32[]{:S(2)}) collective-permute-start(bf16[64,128]{1,0:T(8,128)(2,1)S(1)} %get-tuple-element.31), channel_id=1, source_target_pairs={{0,4},{4,8},{8,12},{12,16},{16,20},{20,24},{24,28},{1,5},{5,9},{9,... | collective-permute-start | bytes 49160 | tf_op jit(solution)/shard_map/ppermute | solution.py:560
  6.5 0.6 copy-start.9
  6.6 0.6 copy-start.10
  27.6 12.4 %collective-permute-start.2 = (bf16[400,128]{1,0:T(8,128)(2,1)}, bf16[400,128]{1,0:T(8,128)(2,1)S(1)}, u32[]{:S(2)}, u32[]{:S(2)}) collective-permute-start(bf16[400,128]{1,0:T(8,128)(2,1)} %get-tuple-element.17), channel_id=1, source_target_pairs={{0,4},{4,8},{8,12},{12,16},{16,20},{20,24},{24,28},{1,5},{5,9},{9,... | collective-permute-start | bytes 307208 | tf_op jit(solution)/shard_map/ppermute | solution.py:566
  32.1 7.9 %copy-start.4 = (bf16[128,768]{1,0:T(8,128)(2,1)S(1)}, bf16[128,768]{1,0:T(8,128)(2,1)}, u32[]{:S(2)}) copy-start(bf16[128,768]{1,0:T(8,128)(2,1)} %weight_ref.4) | copy-start | bytes 589828
  40.0 1.3 %copy-start.2 = (f32[384,768]{1,0:T(8,128)S(1)}, f32[384,768]{1,0:T(8,128)}, u32[]{:S(2)}) copy-start(f32[384,768]{1,0:T(8,128)} %get-tuple-element.18.sum_ref) | copy-start | bytes 3538948
  41.3 0.9 copy-start.5
  43.3 11.6 %collective-permute-start.3 = (bf16[384,768]{1,0:T(8,128)(2,1)S(1)}, bf16[384,768]{1,0:T(8,128)(2,1)S(1)}, u32[]{:S(2)}, u32[]{:S(2)}) collective-permute-start(bf16[384,768]{1,0:T(8,128)(2,1)S(1)} %get-tuple-element.20), channel_id=1, source_target_pairs={{0,8},{9,1},{18,26},{27,19},{4,20},{13,29},{22,6},{31,15}} | collective-permute-start | bytes 1769480 | tf_op jit(solution)/shard_map/ppermute | solution.py:530
  55.0 8.7 %collective-permute-start.4 = (bf16[384,768]{1,0:T(8,128)(2,1)S(1)}, bf16[384,768]{1,0:T(8,128)(2,1)}, u32[]{:S(2)}, u32[]{:S(2)}) collective-permute-start(bf16[384,768]{1,0:T(8,128)(2,1)S(1)} %broadcast_select_fusion), channel_id=1, source_target_pairs={{0,16},{8,24},{1,17},{9,25},{18,2},{26,10},{19,3},{27,11},{4,12},{... | collective-permute-start | bytes 1769480 | tf_op jit(solution)/shard_map/ppermute | solution.py:530
  63.8 1.6 %copy-start.7 = (bf16[384,768]{1,0:T(8,128)(2,1)}, bf16[384,768]{1,0:T(8,128)(2,1)S(1)}, u32[]{:S(2)}) copy-start(bf16[384,768]{1,0:T(8,128)(2,1)S(1)} %broadcast_select_fusion.1.own_ref) | copy-start | bytes 1769476
  63.8 2.1 %collective-permute-start.5 = (bf16[384,768]{1,0:T(8,128)(2,1)S(1)}, bf16[384,768]{1,0:T(8,128)(2,1)S(1)}, u32[]{:S(2)}, u32[]{:S(2)}) collective-permute-start(bf16[384,768]{1,0:T(8,128)(2,1)S(1)} %broadcast_select_fusion.1.own_ref), channel_id=1, source_target_pairs={{0,4},{4,0},{8,12},{12,8},{16,20},{20,16},{24,28},{28,24},{1,5},{5... | collective-permute-start | bytes 1769480 | tf_op jit(solution)/shard_map/ppermute | solution.py:533
  65.9 0.8 copy-start.8
  77.9 12.8 %collective-permute-start.6 = (bf16[192,896]{1,0:T(8,128)(2,1)}, bf16[192,896]{1,0:T(8,128)(2,1)S(1)}, u32[]{:S(2)}, u32[]{:S(2)}) collective-permute-start(bf16[192,896]{1,0:T(8,128)(2,1)} %get-tuple-element.25), channel_id=1, source_target_pairs={{0,1},{1,0},{2,3},{3,2},{4,5},{5,4},{6,7},{7,6},{8,9},{9,8},{10,11... | collective-permute-start | bytes 1032200 | tf_op jit(solution)/shard_map/ppermute | solution.py:577
  81.9 32.2 %copy-start.1 = (bf16[768,768]{1,0:T(8,128)(2,1)S(1)}, bf16[768,768]{1,0:T(8,128)(2,1)}, u32[]{:S(2)}) copy-start(bf16[768,768]{1,0:T(8,128)(2,1)} %weight_ref.5) | copy-start | bytes 3538948
  90.7 1.1 copy-start.3
  91.7 0.9 copy-start.6
  93.1 21.0 %collective-permute-start.7 = (bf16[192,896]{1,0:T(8,128)(2,1)S(1)}, bf16[192,896]{1,0:T(8,128)(2,1)S(1)}, u32[]{:S(2)}, u32[]{:S(2)}) collective-permute-start(bf16[192,896]{1,0:T(8,128)(2,1)S(1)} %get-tuple-element.28), channel_id=1, source_target_pairs={{0,2},{1,3},{2,0},{3,1},{4,6},{5,7},{6,4},{7,5},{8,10},{9,11},{10,... | collective-permute-start | bytes 1032200 | tf_op jit(solution)/shard_map/ppermute | solution.py:581
  114.9 8.1 %collective-permute-start.8 = (bf16[192,768]{1,0:T(8,128)(2,1)S(1)}, bf16[192,768]{1,0:T(8,128)(2,1)S(1)}, u32[]{:S(2)}, u32[]{:S(2)}) collective-permute-start(bf16[192,768]{1,0:T(8,128)(2,1)S(1)} %merge_last.1.own_ref), channel_id=1, source_target_pairs={{0,1},{1,0},{2,3},{3,2},{4,5},{5,4},{6,7},{7,6},{8,9},{9,8},{10,11... | collective-permute-start | bytes 884744 | tf_op jit(solution)/shard_map/ppermute | solution.py:583
where the time goes:
time: 124 us
  Pallas kernels  50.8 us (41%)
  waiting for transfers between devices  37.8 us (30%)
  starting transfers between devices  25.8 us (21%)
  local copies, waits for them, and re-layouts  7.12 us (6%)
  matrix products  1.44 us (1%)
    pallas_call x1, Pallas kernels, atom_attention(): pl.pallas_call(functools.partial(atom_kernel, chunks, atom_total, tok_row...  20.4 us
    ppermute x1, waiting for transfers between devices, body(): got = lax.ppermute(far, 'ka', [(i, i ^ bit) for i in range(n_ka)])  15.2 us
    ppermute x2, waiting for transfers between devices, key_block(): moved = lax.ppermute(held, ('pb', 'ka'), pairs)  13.8 us
    pallas_call x1, Pallas kernels, attention(): pl.pallas_call(functools.partial(send_kernel, steps), grid_spec=pltpu.Pre...  11.2 us
    pallas_call x1, Pallas kernels, attention(): pl.pallas_call(keep_kernel, grid_spec=pltpu.PrefetchScalarGridSpec(num_sc...  8.06 us
    pallas_call x1, Pallas kernels, pool(): pl.pallas_call(functools.partial(pool_kernel, tok_rows), grid_spec=pltpu....  7.9 us
    ppermute x1, waiting for transfers between devices, body(): rest = lax.ppermute(part, 'ka', [(i, i ^ 1) for i in range(n_ka)])  7.37 us
    ppermute x2, starting transfers between devices, key_block(): moved = lax.ppermute(held, ('pb', 'ka'), pairs)  6.43 us
  transfers between devices with their start and end apart: 9, of which 7 were waited for; matrix products, arithmetic and copies ran while one was open for 2% of the time, Pallas kernels for 13%

commit v1 on v0

--- a/solution.py
+++ b/solution.py
@@ -71,7 +71,7 @@
 
     @pl.when(step == 0)
     def _():
-        gain = gain_ref[...]
+        gain = gain_ref[...].reshape(1, width)
 
         def project(values):
             normed = norm_rows(values.astype(F32), gain).astype(BF16)
@@ -171,7 +171,7 @@
                 full((rows, width)),
                 full((half, width)),
                 full((half, width)),
-                full((1, width)),
+                full((width,)),
                 full(qkv.shape),
                 full(proj.shape),
                 pl.BlockSpec((AH, size, WIN_K), lambda i, *_: (0, i, 0)),
@@ -270,7 +270,7 @@
     sums = sum_ref[...] + dot(hot, hidden)
     token_repr = (sums / jnp.sum(count, axis=1, keepdims=True)).astype(BF16)
     repr_ref[...] = token_repr
-    normed_ref[...] = norm_rows(token_repr.astype(F32), gain_ref[...]).astype(BF16)
+    normed_ref[...] = norm_rows(token_repr.astype(F32), gain_ref[...].reshape(1, -1)).astype(BF16)
 
 
 def finish(msg, weight, sums, counts, gain):
@@ -305,44 +305,76 @@
     return value + pltpu.roll(value, LANES - TH, 1) + pltpu.roll(value, LANES - 2 * TH, 1)
 
 
-def attend_step(step, half, q_ref, k_ref, v_ref, bias_ref, o_s, lse_s):
+ROW_TILE = 32
+
+
+def attend_step(step, half, q_ref, k_ref, v_ref, bias_ref, o_s, lse_s, work):
     rows = o_s.shape[0]
     width = q_ref.shape[1] // TH
     span = HEADS_STEP * width
     at = pl.multiple_of(half * rows, rows)
     spot = lax.broadcasted_iota(jnp.int32, (rows, LANES), 1)
-    lse = lse_s[...]
-    for p in range(HEADS_STEP // 2):
+    pairs = HEADS_STEP // 2
+    score_s, term_s, top_s = work[:2], work[2:4], work[4:]
+
+    def layout(p):
         first = 2 * p * width
         low = first // LANES * LANES
         wide = -(-(first + 2 * width) // LANES) * LANES - low
+        lane = lax.broadcasted_iota(jnp.int32, (rows, wide), 1)
         first -= low
-        free = 0 if first >= 16 else 2 * width
-        window = pl.ds(pl.multiple_of(step * span + low, LANES), wide)
-        lane = lax.broadcasted_iota(jnp.int32, (rows, wide), 1)
         masks = [(lane >= first + j * width) & (lane < first + (j + 1) * width) for j in range(2)]
+        return pl.ds(pl.multiple_of(step * span + low, LANES), wide), first, masks
+
+    def score(p):
+        window, _, masks = layout(p)
         query = q_ref[pl.ds(at, rows), window].astype(F32)
         stacked = jnp.concatenate([jnp.where(m, query, 0.0).astype(BF16) for m in masks], axis=0)
-        bias = bias_ref[2 * p : 2 * p + 2].astype(F32)
-        scores = dot_nt(stacked, k_ref[:, window]) + bias.reshape(2 * rows, bias.shape[2])
-        top = jnp.max(scores, axis=-1, keepdims=True)
-        terms = jnp.exp(scores - top).astype(BF16)
+        score_s[p % 2][...] = dot_nt(stacked, k_ref[:, window])
+
+    def soften(p):
+        for r in range(0, 2 * rows, ROW_TILE):
+            bias = bias_ref[2 * p + r // rows, r % rows : r % rows + ROW_TILE, :].astype(F32)
+            scores = score_s[p % 2][r : r + ROW_TILE, :] + bias
+            top = jnp.max(scores, axis=-1, keepdims=True)
+            term_s[p % 2][r : r + ROW_TILE, :] = jnp.exp(scores - top).astype(BF16)
+            top_s[p % 2][r : r + ROW_TILE, :] = jnp.broadcast_to(top, (ROW_TILE, LANES))
+
+    def mix(p):
+        window, first, masks = layout(p)
         values = v_ref[:, window]
         column = lax.broadcasted_iota(jnp.int32, values.shape, 1)
         used = (column >= first) & (column < first + 2 * width)
-        mixed = dot(terms, jnp.where(used, values.astype(F32), 1.0).astype(BF16))
+        mixed = dot(term_s[p % 2][...], jnp.where(used, values.astype(F32), 1.0).astype(BF16))
+        free = 0 if first >= 16 else 2 * width
         total = mixed[:, free : free + 1]
         mixed = mixed / total
-        sums = top + jnp.log(total)
+        sums = top_s[p % 2][...] + jnp.log(total)
         result = o_s[:, window]
+        lse = lse_s[...]
         for j in range(2):
             result = jnp.where(masks[j], mixed[j * rows : (j + 1) * rows], result)
             lse = jnp.where(spot == step * HEADS_STEP + 2 * p + j, sums[j * rows : (j + 1) * rows], lse)
         o_s[:, window] = result
-    lse_s[...] = lse
-
-
-def send_kernel(steps, half_ref, core_ref, q_ref, own_ref, other_ref, wkv_ref, bias_ref, k_ref, v_ref, msg_ref, o_s, lse_s, x_s):
+        lse_s[...] = lse
+
+    score(0)
+    for p in range(pairs):
+        if p + 1 < pairs:
+            score(p + 1)
+        soften(p)
+        mix(p)
+
+
+def work_scratch(rows, keys):
+    return (
+        [pltpu.VMEM((2 * rows, keys), F32)] * 2
+        + [pltpu.VMEM((2 * rows, keys), BF16)] * 2
+        + [pltpu.VMEM((2 * rows, LANES), F32)] * 2
+    )
+
+
+def send_kernel(steps, half_ref, core_ref, q_ref, own_ref, other_ref, wkv_ref, bias_ref, k_ref, v_ref, msg_ref, o_s, lse_s, x_s, *work):
     step = pl.program_id(0)
     rows, feats = own_ref.shape
 
@@ -356,7 +388,7 @@
             v_ref[r : r + rows, :] = dot(x_s[r : r + rows, :], wkv_ref[:, feats:]).astype(BF16)
         lse_s[...] = jnp.zeros_like(lse_s)
 
-    attend_step(step, half_ref[0], q_ref, k_ref, v_ref, bias_ref, o_s, lse_s)
+    attend_step(step, half_ref[0], q_ref, k_ref, v_ref, bias_ref, o_s, lse_s, work)
 
     @pl.when(step == steps - 1)
     def _():
@@ -364,14 +396,14 @@
         msg_ref[:, feats:] = pack_lse(lse_s[...])
 
 
-def keep_kernel(half_ref, q_ref, k_ref, v_ref, bias_ref, o_ref, lse_ref):
+def keep_kernel(half_ref, q_ref, k_ref, v_ref, bias_ref, o_ref, lse_ref, *work):
     step = pl.program_id(0)
 
     @pl.when(step == 0)
     def _():
         lse_ref[...] = jnp.zeros_like(lse_ref)
 
-    attend_step(step, half_ref[0], q_ref, k_ref, v_ref, bias_ref, o_ref, lse_ref)
+    attend_step(step, half_ref[0], q_ref, k_ref, v_ref, bias_ref, o_ref, lse_ref, work)
 
 
 def attention(half, q, bias, keys, first):
@@ -395,6 +427,7 @@
                     pltpu.VMEM((rows, feats), F32),
                     pltpu.VMEM((rows, LANES), F32),
                     pltpu.VMEM(kv_shape, BF16),
+                    *work_scratch(rows, key_rows),
                 ],
             ),
             out_shape=[
@@ -414,6 +447,7 @@
             grid=(steps,),
             in_specs=[full(q.shape), full(kv_shape), full(kv_shape), bias_spec],
             out_specs=[full((rows, feats)), full((rows, LANES))],
+            scratch_shapes=work_scratch(rows, key_rows),
         ),
         out_shape=[
             jax.ShapeDtypeStruct((rows, feats), F32),
@@ -560,16 +594,16 @@
     left = lax.ppermute(atoms[rows - half :], "pb", up)
     right = lax.ppermute(atoms[:half], "pb", down)
     atom_out, msg = atom_attention(
-        window_shift, pos, atoms, left, right, atom_gain.reshape(1, width), atom_qkv, atom_proj,
+        window_shift, pos, atoms, left, right, atom_gain, atom_qkv, atom_proj,
         atom_bias, tok2d, tok_rows, rows * n_pb,
     )
     behind = lax.ppermute(msg, "pb", up)
     sums, counts = pool(pos, atom_out, agg_weight, tok2d, tok_rows)
-    token_repr, normed = finish(behind, agg_weight, sums, counts, token_gain.reshape(1, -1))
+    token_repr, normed = finish(behind, agg_weight, sums, counts, token_gain)
     own_keys, other_keys = key_block(normed)
     scale = 1.0 / math.sqrt(token_q.shape[1] // TH)
     queries = (dot(normed, token_q) * scale).astype(BF16)
-    parity = lax.rem(plane, 2).astype(jnp.int32)
+    parity = jnp.bitwise_and(plane ^ (plane >> 1), 1).astype(jnp.int32)
     core = lax.rem(shard, n_pb // n_ka).astype(jnp.int32)
     k, v, near = attention(
         (1 - parity).reshape(1), queries, pair_bias, (core.reshape(1), own_keys, other_keys, token_kv), True
@@ -578,7 +612,7 @@
     o, lse = attention(parity.reshape(1), queries, pair_bias, (k, v), False)
     for bit in bits_of(n_ka)[1:]:
         o, lse, far = merge(o, lse, got)
-        got = lax.ppermute(far, "ka", [(i, i ^ bit) for i in range(n_ka)])
+        got = lax.ppermute(far, "ka", [(i, i ^ (2 * bit - 1)) for i in range(n_ka)])
     part = last_merge(parity.reshape(1), o, lse, got, token_repr, token_o)
     rest = lax.ppermute(part, "ka", [(i, i ^ 1) for i in range(n_ka)])
     return atom_out, join(parity.reshape(1), part, rest)

time: 124 us -> 123 us (level)
  waiting for transfers between devices: 37.8 us -> 31 us
  starting transfers between devices: 25.8 us -> 31.4 us
    ppermute x1, waiting for transfers between devices: 15.2 us -> 7.65 us  [body(): got = lax.ppermute(far, 'ka', [(i, i ^ 2 * bit - 1) for i in range(n_ka)])]
    ppermute x1, starting transfers between devices: 0.75 us -> 7.03 us  [body(): rest = lax.ppermute(part, 'ka', [(i, i ^ 1) for i in range(n_ka)])]
  transfers between devices with their start and end apart: 9 -> 9, of which waited for: 7 -> 7; matrix products, arithmetic and copies ran while one was open for 2% -> 1% of each run, Pallas kernels for 13% -> 13%
where the time goes in v1:
time: 123 us; the launch traced here: 122 us
  Pallas kernels  50.2 us (41%)
  starting transfers between devices  31.4 us (26%)
  waiting for transfers between devices  31 us (25%)
  local copies, waits for them, and re-layouts  6.43 us (5%)
  matrix products  1.44 us (1%)
    pallas_call x1, Pallas kernels, atom_attention(): pl.pallas_call(functools.partial(atom_kernel, chunks, atom_total, tok_row...  20.4 us
    ppermute x2, waiting for transfers between devices, key_block(): moved = lax.ppermute(held, ('pb', 'ka'), pairs)  14.5 us
    pallas_call x1, Pallas kernels, attention(): pl.pallas_call(functools.partial(send_kernel, steps), grid_spec=pltpu.Pre...  11 us
    pallas_call x1, Pallas kernels, pool(): pl.pallas_call(functools.partial(pool_kernel, tok_rows), grid_spec=pltpu....  7.92 us
    pallas_call x1, Pallas kernels, attention(): pl.pallas_call(keep_kernel, grid_spec=pltpu.PrefetchScalarGridSpec(num_sc...  7.72 us
    ppermute x1, waiting for transfers between devices, body(): got = lax.ppermute(far, 'ka', [(i, i ^ 2 * bit - 1) for i in range(n_ka)])  7.65 us
    ppermute x1, starting transfers between devices, body(): rest = lax.ppermute(part, 'ka', [(i, i ^ 1) for i in range(n_ka)])  7.03 us
    ppermute x1, starting transfers between devices, body(): got = lax.ppermute(far, 'ka', [(i, i ^ 2 * bit - 1) for i in range(n_ka)])  6.94 us
  transfers between devices with their start and end apart: 9, of which 7 were waited for; matrix products, arithmetic and copies ran while one was open for 1% of the time, Pallas kernels for 13%

profile of v1, /device:TPU:0, one launch (start us, length us, event | category | flops | bytes accessed | tf_op | source)
XLA Modules:
  0.0 122.3 jit_solution(6727679964460305024)
XLA Ops:
  0.6 0.8 fusion.1
  1.5 1.3 %collective-permute-start.1 = (bf16[64,128]{1,0:T(8,128)(2,1)S(1)}, bf16[64,128]{1,0:T(8,128)(2,1)S(1)}, u32[]{:S(2)}, u32[]{:S(2)}) collective-permute-start(bf16[64,128]{1,0:T(8,128)(2,1)S(1)} %get-tuple-element.30), channel_id=1, source_target_pairs={{4,0},{8,4},{12,8},{16,12},{20,16},{24,20},{28,24},{5,1},{9,5},{13... | collective-permute-start | bytes 49160 | tf_op jit(solution)/shard_map/ppermute | solution.py:595
  2.8 3.0 %collective-permute-start = (bf16[64,128]{1,0:T(8,128)(2,1)S(1)}, bf16[64,128]{1,0:T(8,128)(2,1)S(1)}, u32[]{:S(2)}, u32[]{:S(2)}) collective-permute-start(bf16[64,128]{1,0:T(8,128)(2,1)S(1)} %get-tuple-element.31), channel_id=1, source_target_pairs={{0,4},{4,8},{8,12},{12,16},{16,20},{20,24},{24,28},{1,5},{5,9},{9,... | collective-permute-start | bytes 49160 | tf_op jit(solution)/shard_map/ppermute | solution.py:594
  5.8 0.8 collective-permute-done.left_ref
  6.6 0.6 copy-done.10
  7.2 20.4 %atom_attention.1 = (bf16[3072,128]{1,0:T(8,128)(2,1)}, bf16[400,128]{1,0:T(8,128)(2,1)}) custom-call(s32[96]{0:T(128)} %shift_ref.1, s32[1]{0:T(128)} %bitcast.pos_ref, bf16[3072,128]{1,0:T(8,128)(2,1)} %atoms_ref.1, bf16[64,128]{1,0:T(8,128)(2,1)} %copy-done.10, bf16[64,128]{1,0:T(8,128)(2,1)} %copy-done.9, f32[128]{0:T(128)} %gain_ref.2, ...), custom_call_target="tpu_custom_call" | custom-call | flops 8000000000 | bytes 6000000 | tf_op jit(solution)/shard_map/atom_attention/pallas_call | solution.py:165
  27.6 4.5 %collective-permute-start.2 = (bf16[400,128]{1,0:T(8,128)(2,1)}, bf16[400,128]{1,0:T(8,128)(2,1)S(1)}, u32[]{:S(2)}, u32[]{:S(2)}) collective-permute-start(bf16[400,128]{1,0:T(8,128)(2,1)} %get-tuple-element.17), channel_id=1, source_target_pairs={{0,4},{4,8},{8,12},{12,16},{16,20},{20,24},{24,28},{1,5},{5,9},{9,... | collective-permute-start | bytes 307208 | tf_op jit(solution)/shard_map/ppermute | solution.py:600
  32.1 7.9 %pool.1 = (f32[384,768]{1,0:T(8,128)}, f32[384,128]{1,0:T(8,128)}) custom-call(s32[1]{0:T(128)} %bitcast.pos_ref, bf16[3072,128]{1,0:T(8,128)(2,1)} %get-tuple-element.14.out_ref, bf16[128,768]{1,0:T(8,128)(2,1)} %weight_ref.4, s32[24,128]{1,0:T(8,128)} %bitcast.8), custom_call_target="tpu_custom_call" | custom-call | flops 4000000000 | bytes 3000000 | tf_op jit(solution)/shard_map/pool/pallas_call | solution.py:236
  40.1 1.3 %copy-done.2 = f32[384,768]{1,0:T(8,128)S(1)} copy-done((f32[384,768]{1,0:T(8,128)S(1)}, f32[384,768]{1,0:T(8,128)}, u32[]{:S(2)}) %copy-start.2) | copy-done | bytes 1179672
  41.3 0.9 copy-done.5
  42.2 1.1 token_finish.1
  43.4 4.3 %collective-permute-start.3 = (bf16[384,768]{1,0:T(8,128)(2,1)S(1)}, bf16[384,768]{1,0:T(8,128)(2,1)S(1)}, u32[]{:S(2)}, u32[]{:S(2)}) collective-permute-start(bf16[384,768]{1,0:T(8,128)(2,1)S(1)} %get-tuple-element.20), channel_id=1, source_target_pairs={{0,8},{9,1},{18,26},{27,19},{4,20},{13,29},{22,6},{31,15}} | collective-permute-start | bytes 1769480 | tf_op jit(solution)/shard_map/ppermute | solution.py:564
  47.7 7.3 %collective-permute-done.3 = bf16[384,768]{1,0:T(8,128)(2,1)S(1)} collective-permute-done((bf16[384,768]{1,0:T(8,128)(2,1)S(1)}, bf16[384,768]{1,0:T(8,128)(2,1)S(1)}, u32[]{:S(2)}, u32[]{:S(2)}) %collective-permute-start.3) | collective-permute-done | bytes 589856 | tf_op jit(solution)/shard_map/ppermute | solution.py:564
  55.1 1.5 %collective-permute-start.4 = (bf16[384,768]{1,0:T(8,128)(2,1)S(1)}, bf16[384,768]{1,0:T(8,128)(2,1)S(1)}, u32[]{:S(2)}, u32[]{:S(2)}) collective-permute-start(bf16[384,768]{1,0:T(8,128)(2,1)S(1)} %broadcast_select_fusion), channel_id=1, source_target_pairs={{0,16},{8,24},{1,17},{9,25},{18,2},{26,10},{19,3},{27,11},{4,12},{... | collective-permute-start | bytes 1769480 | tf_op jit(solution)/shard_map/ppermute | solution.py:564
  56.6 7.1 %collective-permute-done.4 = bf16[384,768]{1,0:T(8,128)(2,1)S(1)} collective-permute-done((bf16[384,768]{1,0:T(8,128)(2,1)S(1)}, bf16[384,768]{1,0:T(8,128)(2,1)S(1)}, u32[]{:S(2)}, u32[]{:S(2)}) %collective-permute-start.4) | collective-permute-done | bytes 589856 | tf_op jit(solution)/shard_map/ppermute | solution.py:564
  63.8 0.9 broadcast_select_fusion.1.own_ref
  64.7 1.4 %fusion.q_ref = bf16[384,768]{1,0:T(8,128)(2,1)} fusion(bf16[384,768]{1,0:T(8,128)(2,1)S(1)} %get-tuple-element.20, bf16[768,768]{1,0:T(8,128)(2,1)S(1)} %copy-done), kind=kOutput, calls=%fused_computation.1 | convolution fusion | flops 453574656 | bytes 2359296 | tf_op jit(solution)/shard_map/dot_general | solution.py:38
  66.1 0.7 collective-permute-done.5.other_ref
  66.9 0.8 copy-done.8
  67.7 11.0 %attend_send.1 = (bf16[768,768]{1,0:T(8,128)(2,1)}, bf16[768,768]{1,0:T(8,128)(2,1)}, bf16[192,896]{1,0:T(8,128)(2,1)}) custom-call(s32[1]{0:T(128)} %bitcast.3.half_ref, s32[1]{0:T(128)} %bitcast.4.core_ref, bf16[384,768]{1,0:T(8,128)(2,1)} %fusion.q_ref, bf16[384,768]{1,0:T(8,128)(2,1)} %broadcast_select_fusion.1.own_ref, bf16[384,768]{1,0:T(8,128)(2,1)} %copy-done.8, ...), custom_call_target="tpu_custom_call" | custom-call | flops 8000000000 | bytes 8000000 | tf_op jit(solution)/shard_map/attend_send/pallas_call | solution.py:419
  78.6 2.8 %collective-permute-start.6 = (bf16[192,896]{1,0:T(8,128)(2,1)}, bf16[192,896]{1,0:T(8,128)(2,1)S(1)}, u32[]{:S(2)}, u32[]{:S(2)}) collective-permute-start(bf16[192,896]{1,0:T(8,128)(2,1)} %get-tuple-element.25), channel_id=1, source_target_pairs={{0,1},{1,0},{2,3},{3,2},{4,5},{5,4},{6,7},{7,6},{8,9},{9,8},{10,11... | collective-permute-start | bytes 1032200 | tf_op jit(solution)/shard_map/ppermute | solution.py:611
  81.5 7.7 %attend_keep.1 = (f32[192,768]{1,0:T(8,128)}, f32[192,128]{1,0:T(8,128)}) custom-call(s32[1]{0:T(128)} %bitcast.2.half_ref, bf16[384,768]{1,0:T(8,128)(2,1)} %fusion.q_ref, bf16[768,768]{1,0:T(8,128)(2,1)} %get-tuple-element.21.k_ref, bf16[768,768]{1,0:T(8,128)(2,1)} %get-tuple-element.22.v_ref, bf16[16,384,768]{2,1,0:T(8,128)(2,1)} %bias_ref.5), custom_call_target="tpu_custom_call" | custom-call | flops 8000000000 | bytes 8000000 | tf_op jit(solution)/shard_map/attend_keep/pallas_call | solution.py:443
  89.2 1.1 collective-permute-done.6.msg_ref
  90.2 1.1 copy-done.3
  91.3 0.9 copy-done.6
  92.2 0.5 merge.1
  92.7 6.9 %collective-permute-start.7 = (bf16[192,896]{1,0:T(8,128)(2,1)S(1)}, bf16[192,896]{1,0:T(8,128)(2,1)S(1)}, u32[]{:S(2)}, u32[]{:S(2)}) collective-permute-start(bf16[192,896]{1,0:T(8,128)(2,1)S(1)} %get-tuple-element.28), channel_id=1, source_target_pairs={{0,3},{1,2},{2,1},{3,0},{4,7},{5,6},{6,5},{7,4},{8,11},{9,10},{10,... | collective-permute-start | bytes 1032200 | tf_op jit(solution)/shard_map/ppermute | solution.py:615
  99.6 7.6 %collective-permute-done.7.msg_ref = bf16[192,896]{1,0:T(8,128)(2,1)S(1)} collective-permute-done((bf16[192,896]{1,0:T(8,128)(2,1)S(1)}, bf16[192,896]{1,0:T(8,128)(2,1)S(1)}, u32[]{:S(2)}, u32[]{:S(2)}) %collective-permute-start.7) | collective-permute-done | bytes 344096 | tf_op jit(solution)/shard_map/ppermute | solution.py:615
  107.3 0.8 merge_last.1.own_ref
  108.1 7.0 %collective-permute-start.8 = (bf16[192,768]{1,0:T(8,128)(2,1)S(1)}, bf16[192,768]{1,0:T(8,128)(2,1)S(1)}, u32[]{:S(2)}, u32[]{:S(2)}) collective-permute-start(bf16[192,768]{1,0:T(8,128)(2,1)S(1)} %merge_last.1.own_ref), channel_id=1, source_target_pairs={{0,1},{1,0},{2,3},{3,2},{4,5},{5,4},{6,7},{7,6},{8,9},{9,8},{10,11... | collective-permute-start | bytes 884744 | tf_op jit(solution)/shard_map/ppermute | solution.py:617
  115.1 6.3 %collective-permute-done.8.other_ref = bf16[192,768]{1,0:T(8,128)(2,1)S(1)} collective-permute-done((bf16[192,768]{1,0:T(8,128)(2,1)S(1)}, bf16[192,768]{1,0:T(8,128)(2,1)S(1)}, u32[]{:S(2)}, u32[]{:S(2)}) %collective-permute-start.8) | collective-permute-done | bytes 294944 | tf_op jit(solution)/shard_map/ppermute | solution.py:617
  121.4 0.9 join.1
  (20 shorter events, 0.1 us)
Async XLA Ops:
  0.6 64.0 %copy-start = (bf16[768,768]{1,0:T(8,128)(2,1)S(1)}, bf16[768,768]{1,0:T(8,128)(2,1)}, u32[]{:S(2)}) copy-start(bf16[768,768]{1,0:T(8,128)(2,1)} %param.22) | copy-start | bytes 3538948
  1.5 4.3 %collective-permute-start.1 = (bf16[64,128]{1,0:T(8,128)(2,1)S(1)}, bf16[64,128]{1,0:T(8,128)(2,1)S(1)}, u32[]{:S(2)}, u32[]{:S(2)}) collective-permute-start(bf16[64,128]{1,0:T(8,128)(2,1)S(1)} %get-tuple-element.30), channel_id=1, source_target_pairs={{4,0},{8,4},{12,8},{16,12},{20,16},{24,20},{28,24},{5,1},{9,5},{13... | collective-permute-start | bytes 49160 | tf_op jit(solution)/shard_map/ppermute | solution.py:595
  2.8 3.9 %collective-permute-start = (bf16[64,128]{1,0:T(8,128)(2,1)S(1)}, bf16[64,128]{1,0:T(8,128)(2,1)S(1)}, u32[]{:S(2)}, u32[]{:S(2)}) collective-permute-start(bf16[64,128]{1,0:T(8,128)(2,1)S(1)} %get-tuple-element.31), channel_id=1, source_target_pairs={{0,4},{4,8},{8,12},{12,16},{16,20},{20,24},{24,28},{1,5},{5,9},{9,... | collective-permute-start | bytes 49160 | tf_op jit(solution)/shard_map/ppermute | solution.py:594
  5.8 0.8 copy-start.9
  6.6 0.6 copy-start.10
  27.6 12.4 %collective-permute-start.2 = (bf16[400,128]{1,0:T(8,128)(2,1)}, bf16[400,128]{1,0:T(8,128)(2,1)S(1)}, u32[]{:S(2)}, u32[]{:S(2)}) collective-permute-start(bf16[400,128]{1,0:T(8,128)(2,1)} %get-tuple-element.17), channel_id=1, source_target_pairs={{0,4},{4,8},{8,12},{12,16},{16,20},{20,24},{24,28},{1,5},{5,9},{9,... | collective-permute-start | bytes 307208 | tf_op jit(solution)/shard_map/ppermute | solution.py:600
  32.1 7.9 %copy-start.4 = (bf16[128,768]{1,0:T(8,128)(2,1)S(1)}, bf16[128,768]{1,0:T(8,128)(2,1)}, u32[]{:S(2)}) copy-start(bf16[128,768]{1,0:T(8,128)(2,1)} %weight_ref.4) | copy-start | bytes 589828
  32.1 7.9 %copy-start.7 = (f32[768]{0:T(1024)S(1)}, f32[768]{0:T(1024)}, u32[]{:S(2)}) copy-start(f32[768]{0:T(1024)} %gain_ref.3) | copy-start | bytes 9220
  40.0 1.3 %copy-start.2 = (f32[384,768]{1,0:T(8,128)S(1)}, f32[384,768]{1,0:T(8,128)}, u32[]{:S(2)}) copy-start(f32[384,768]{1,0:T(8,128)} %get-tuple-element.18.sum_ref) | copy-start | bytes 3538948
  41.3 0.9 copy-start.5
  43.4 11.7 %collective-permute-start.3 = (bf16[384,768]{1,0:T(8,128)(2,1)S(1)}, bf16[384,768]{1,0:T(8,128)(2,1)S(1)}, u32[]{:S(2)}, u32[]{:S(2)}) collective-permute-start(bf16[384,768]{1,0:T(8,128)(2,1)S(1)} %get-tuple-element.20), channel_id=1, source_target_pairs={{0,8},{9,1},{18,26},{27,19},{4,20},{13,29},{22,6},{31,15}} | collective-permute-start | bytes 1769480 | tf_op jit(solution)/shard_map/ppermute | solution.py:564
  55.1 8.7 %collective-permute-start.4 = (bf16[384,768]{1,0:T(8,128)(2,1)S(1)}, bf16[384,768]{1,0:T(8,128)(2,1)S(1)}, u32[]{:S(2)}, u32[]{:S(2)}) collective-permute-start(bf16[384,768]{1,0:T(8,128)(2,1)S(1)} %broadcast_select_fusion), channel_id=1, source_target_pairs={{0,16},{8,24},{1,17},{9,25},{18,2},{26,10},{19,3},{27,11},{4,12},{... | collective-permute-start | bytes 1769480 | tf_op jit(solution)/shard_map/ppermute | solution.py:564
  64.6 2.2 %collective-permute-start.5 = (bf16[384,768]{1,0:T(8,128)(2,1)}, bf16[384,768]{1,0:T(8,128)(2,1)S(1)}, u32[]{:S(2)}, u32[]{:S(2)}) collective-permute-start(bf16[384,768]{1,0:T(8,128)(2,1)} %broadcast_select_fusion.1.own_ref), channel_id=1, source_target_pairs={{0,4},{4,0},{8,12},{12,8},{16,20},{20,16},{24,28},{28,24},{1,5},{5... | collective-permute-start | bytes 1769480 | tf_op jit(solution)/shard_map/ppermute | solution.py:567
  66.8 0.8 copy-start.8
  78.6 11.6 %collective-permute-start.6 = (bf16[192,896]{1,0:T(8,128)(2,1)}, bf16[192,896]{1,0:T(8,128)(2,1)S(1)}, u32[]{:S(2)}, u32[]{:S(2)}) collective-permute-start(bf16[192,896]{1,0:T(8,128)(2,1)} %get-tuple-element.25), channel_id=1, source_target_pairs={{0,1},{1,0},{2,3},{3,2},{4,5},{5,4},{6,7},{7,6},{8,9},{9,8},{10,11... | collective-permute-start | bytes 1032200 | tf_op jit(solution)/shard_map/ppermute | solution.py:611
  81.5 25.8 %copy-start.1 = (bf16[768,768]{1,0:T(8,128)(2,1)S(1)}, bf16[768,768]{1,0:T(8,128)(2,1)}, u32[]{:S(2)}) copy-start(bf16[768,768]{1,0:T(8,128)(2,1)} %weight_ref.5) | copy-start | bytes 3538948
  90.2 1.1 copy-start.3
  91.3 0.9 copy-start.6
  92.7 14.6 %collective-permute-start.7 = (bf16[192,896]{1,0:T(8,128)(2,1)S(1)}, bf16[192,896]{1,0:T(8,128)(2,1)S(1)}, u32[]{:S(2)}, u32[]{:S(2)}) collective-permute-start(bf16[192,896]{1,0:T(8,128)(2,1)S(1)} %get-tuple-element.28), channel_id=1, source_target_pairs={{0,3},{1,2},{2,1},{3,0},{4,7},{5,6},{6,5},{7,4},{8,11},{9,10},{10,... | collective-permute-start | bytes 1032200 | tf_op jit(solution)/shard_map/ppermute | solution.py:615
  108.1 13.4 %collective-permute-start.8 = (bf16[192,768]{1,0:T(8,128)(2,1)S(1)}, bf16[192,768]{1,0:T(8,128)(2,1)S(1)}, u32[]{:S(2)}, u32[]{:S(2)}) collective-permute-start(bf16[192,768]{1,0:T(8,128)(2,1)S(1)} %merge_last.1.own_ref), channel_id=1, source_target_pairs={{0,1},{1,0},{2,3},{3,2},{4,5},{5,4},{6,7},{7,6},{8,9},{9,8},{10,11... | collective-permute-start | bytes 884744 | tf_op jit(solution)/shard_map/ppermute | solution.py:617
